TPU v7x, 512 devices: a whole 4x8x8 slice. The times are simulated.
512 devices in a mesh: tiles: 128 (over z, y, core), bands: 4 (over x).
Axes of the slice: x: 4, y: 8, z: 8, core: 2. Of those that a mesh axis runs over, the one named last changes fastest.
Arguments:
- view_tiles: bfloat16 [12288, 128, 128], P('tiles'), may hold values from 0 to 0.11111111
- vis_rows: int32 [12288], P('tiles'), may hold values from 0 to 2047, as said below
- vis_cols: int32 [12288], P('tiles'), may hold values from 0 to 2047, as said below
- seed_grad: float32 [48, 262144], P('bands', 'tiles'), may hold values from 0.3 to 3
- emissivity: float32 [262144], P('tiles'), may hold values from 0.2 to 0.9
- emissive_power: float32 [48, 262144], P('bands', 'tiles'), may hold values from 0.3 to 4.5
- irradiance: float32 [48, 262144], P('bands', 'tiles'), may hold values from 0.1 to 1
Outputs:
- adjoint: float32 [48, 262144], P('bands', 'tiles')
- emis_grad: float32 [262144], P('tiles')
Inputs may be any that keep to these rules, and one draw needn't show every extreme that they name: `vis_rows`: block k's row tile is owned by the index of tiles that holds block k: it lies from (k // 96) * 16 to (k // 96 + 1) * 16 - 1. `vis_cols`: tile t is owned by index t // 16 of tiles. Among the 96 blocks held by one index of tiles, at most 2 have column tiles owned by any one index; in every draw one index of tiles is named by exactly 2 blocks of every index.
All inputs are finite; a program needn't handle non-finite values.
Results may differ from a plain program's by a relative error of at most 0.00045.
Values may be sent and summed in bfloat16 or wider, within the bound.
A program may use at most 64 MiB of HBM per device.

v0:
```python
import jax
import jax.numpy as jnp
from jax import lax
from jax.sharding import PartitionSpec as P

BANDS = 48
ITERS = 2


def local(view_tiles, vis_rows, vis_cols, seed_grad, emissivity, emissive_power, irradiance):
    patch_width = view_tiles.shape[1]
    devices = lax.axis_size("tiles")
    own_index = lax.axis_index("tiles")
    blocks = view_tiles.shape[0]
    band_count = seed_grad.shape[0]
    tile_count = emissivity.shape[0] // patch_width
    local_rows = vis_rows - own_index * tile_count
    target_device = vis_cols // tile_count
    target_tile = vis_cols - target_device * tile_count
    reflect = (1.0 - emissivity).reshape(tile_count, patch_width)
    seed_tiles = seed_grad.reshape(band_count, tile_count, patch_width)
    capacity = max(2, (2 * blocks + devices - 1) // devices)
    block_order = jnp.arange(blocks, dtype=jnp.int32)
    same_target = (target_device[:, None] == target_device[None, :]) & (
        block_order[None, :] < block_order[:, None]
    )
    slot_rank = jnp.sum(same_target.astype(jnp.int32), axis=1)
    position = target_device * capacity + slot_rank
    slot_tiles = jnp.full((devices * capacity,), -1, jnp.int32).at[position].set(target_tile)
    arrived = lax.all_to_all(
        slot_tiles.reshape(devices, capacity), "tiles", split_axis=0, concat_axis=0, tiled=True
    )
    selector = (
        arrived.reshape(-1)[:, None] == jnp.arange(tile_count, dtype=jnp.int32)[None, :]
    ).astype(jnp.float32)
    adjoint = seed_tiles
    for sweep_index in range(ITERS):
        scaled = (reflect[None] * adjoint).astype(jnp.bfloat16)
        picked = scaled[:, local_rows, :]
        block_terms = jnp.einsum(
            "bkp,kpq->kbq", picked, view_tiles, preferred_element_type=jnp.float32
        )
        packed = (
            jnp.zeros((devices * capacity, band_count, patch_width), jnp.float32)
            .at[position]
            .set(block_terms)
        )
        received = lax.all_to_all(
            packed.reshape(devices, capacity, band_count, patch_width),
            "tiles",
            split_axis=0,
            concat_axis=0,
            tiled=True,
        )
        incoming = jnp.einsum(
            "st,sbp->btp",
            selector,
            received.reshape(devices * capacity, band_count, patch_width),
            precision=lax.Precision.HIGHEST,
            preferred_element_type=jnp.float32,
        )
        adjoint = seed_tiles + incoming
    adjoint_flat = adjoint.reshape(band_count, tile_count * patch_width)
    contrast = emissive_power - irradiance
    partial_grad = jnp.sum(adjoint_flat * contrast, axis=0)
    emis_grad = lax.psum(partial_grad, "bands") / BANDS
    return (adjoint_flat, emis_grad)


def solution(mesh):
    placed = (
        P("tiles", None, None),
        P("tiles"),
        P("tiles"),
        P("bands", "tiles"),
        P("tiles"),
        P("bands", "tiles"),
        P("bands", "tiles"),
    )
    return jax.shard_map(
        local,
        mesh=mesh,
        in_specs=placed,
        out_specs=(P("bands", "tiles"), P("tiles")),
        check_vma=False,
    )
```

profile of v0, /device:TPU:1, one launch (start us, length us, event | category | flops | bytes accessed | tf_op | source)
XLA Modules:
  0.0 182.0 jit_solution(10978330633279471017)
XLA Ops:
  0.6 0.8 multiply_subtract_fusion
  1.6 0.9 scatter_custom_fusion.1
  2.5 0.8 all_to_all.13
  3.3 18.4 %all-to-all-start.1 = ((s32[128,1,2]{2,1,0:T(1,128)}), s32[128,1,2]{2,1,0:T(1,128)S(1)}, u32[]{:S(2)}, u32[]{:S(2)}) async-start(s32[128,1,2]{2,1,0:T(1,128)} %bitcast.4), calls=%async_computation.1 | async-start | bytes 131072 | tf_op jit(solution)/shard_map/all_to_all | solution.py:30
  21.7 0.9 copy.28
  22.7 0.7 subtract_bitcast_fusion
  23.4 0.7 compare_select_fusion
  24.1 1.4 gather_fusion
  25.5 2.8 %fusion.6 = f32[96,12,128]{2,1,0:T(8,128)} fusion(bf16[96,128,128]{2,1,0:T(8,128)(2,1)S(1)} %copy-done, bf16[96,12,128]{2,1,0:T(8,128)(2,1)} %gather_fusion), kind=kOutput, calls=%fused_computation.13 | convolution fusion | flops 37748736 | bytes 4030464 | tf_op jit(solution)/shard_map/bkp,kpq->kbq/dot_general | solution.py:40
  28.3 1.5 broadcast.18.clone
  29.8 11.7 %scatter_fusion = f32[256,12,128]{2,1,0:T(8,128)} fusion(f32[256,12,128]{2,1,0:T(8,128)} %broadcast.18.clone, s32[96]{0:T(128)S(1)} %compare_select_fusion.1, f32[96,12,128]{2,1,0:T(8,128)} %fusion.6), kind=kCustom, calls=%fused_computation.2 | custom fusion | bytes 1769856 | tf_op jit(solution)/shard_map/scatter | solution.py:46
  41.5 3.5 %copy.22 = f32[128,2,12,128]{3,1,2,0:T(2,128)} copy(f32[128,2,12,128]{3,2,1,0:T(8,128)} %bitcast.40) | data formatting | bytes 3145728 | tf_op jit(solution)/shard_map/reshape | solution.py:49
  45.0 14.1 %all-to-all-start = ((f32[128,2,12,128]{3,1,2,0:T(2,128)}), f32[128,2,12,128]{3,1,2,0:T(2,128)}, u32[]{:S(2)}, u32[]{:S(2)}) async-start(f32[128,2,12,128]{3,1,2,0:T(2,128)} %copy.22), calls=%async_computation | async-start | bytes 3145728 | tf_op jit(solution)/shard_map/all_to_all | solution.py:48
  59.7 0.8 reduce.3
  60.7 39.5 %all-to-all-done = f32[128,2,12,128]{3,1,2,0:T(2,128)} async-done(((f32[128,2,12,128]{3,1,2,0:T(2,128)}), f32[128,2,12,128]{3,1,2,0:T(2,128)}, u32[]{:S(2)}, u32[]{:S(2)}) %all-to-all-start) | async-done | bytes 1572896 | tf_op jit(solution)/shard_map/all_to_all | solution.py:48
  100.1 2.1 %copy.23 = f32[128,2,12,128]{3,1,0,2:T(2,128)S(1)} copy(f32[128,2,12,128]{3,1,2,0:T(2,128)} %all-to-all-done) | data formatting | bytes 3145728 | tf_op jit(solution)/shard_map/all_to_all | solution.py:48
  102.9 1.4 gather_fusion.1
  104.3 2.8 %fusion.4 = f32[96,12,128]{2,1,0:T(8,128)} fusion(bf16[96,128,128]{2,1,0:T(8,128)(2,1)S(1)} %copy-done, bf16[96,12,128]{2,1,0:T(8,128)(2,1)} %gather_fusion.1), kind=kOutput, calls=%fused_computation.11 | convolution fusion | flops 37748736 | bytes 4030464 | tf_op jit(solution)/shard_map/bkp,kpq->kbq/dot_general | solution.py:40
  107.2 1.5 broadcast.18
  108.6 11.7 %scatter_fusion.1 = f32[256,12,128]{2,1,0:T(8,128)} fusion(f32[256,12,128]{2,1,0:T(8,128)} %broadcast.18, s32[96]{0:T(128)S(1)} %compare_select_fusion.1, f32[96,12,128]{2,1,0:T(8,128)} %fusion.4), kind=kCustom, calls=%fused_computation.4 | custom fusion | bytes 1769856 | tf_op jit(solution)/shard_map/scatter | solution.py:46
  120.3 2.4 %copy.26 = f32[128,2,12,128]{3,1,2,0:T(2,128)S(1)} copy(f32[128,2,12,128]{3,2,1,0:T(8,128)} %bitcast.39) | data formatting | bytes 3145728 | tf_op jit(solution)/shard_map/reshape | solution.py:49
  122.7 48.5 %all_to_all.19 = f32[128,2,12,128]{3,1,2,0:T(2,128)S(1)} all-to-all(f32[128,2,12,128]{3,1,2,0:T(2,128)S(1)} %copy.26), channel_id=1, replica_groups=mesh['tiles'=128,'bands'=4] {'tiles'}, dimensions={0} | all-to-all | bytes 3145728 | tf_op jit(solution)/shard_map/all_to_all | solution.py:48
  171.3 0.7 copy.27
  172.8 8.6 %psum.7 = f32[2048]{0:T(1024)S(1)} all-reduce(f32[2048]{0:T(1024)S(1)} %multiply_reduce_fusion), channel_id=1, replica_groups=mesh['tiles'=128,'bands'=4] {'bands'}, use_global_device_ids=true, to_apply=%region_5.6 | all-reduce | flops 2048 | bytes 16384 | tf_op jit(solution)/shard_map/psum | solution.py:66
  (23 shorter events, 2.9 us)
Async XLA Ops:
  0.6 24.9 %copy-start = (bf16[96,128,128]{2,1,0:T(8,128)(2,1)S(1)}, bf16[96,128,128]{2,1,0:T(8,128)(2,1)}, u32[]{:S(2)}) copy-start(bf16[96,128,128]{2,1,0:T(8,128)(2,1)} %param.7) | copy-start | bytes 9437188
  3.3 41.7 %all-to-all-start.1 = ((s32[128,1,2]{2,1,0:T(1,128)}), s32[128,1,2]{2,1,0:T(1,128)S(1)}, u32[]{:S(2)}, u32[]{:S(2)}) async-start(s32[128,1,2]{2,1,0:T(1,128)} %bitcast.4), calls=%async_computation.1 | async-start | bytes 131072 | tf_op jit(solution)/shard_map/all_to_all | solution.py:30
  45.0 55.1 %all-to-all-start = ((f32[128,2,12,128]{3,1,2,0:T(2,128)}), f32[128,2,12,128]{3,1,2,0:T(2,128)}, u32[]{:S(2)}, u32[]{:S(2)}) async-start(f32[128,2,12,128]{3,1,2,0:T(2,128)} %copy.22), calls=%async_computation | async-start | bytes 3145728 | tf_op jit(solution)/shard_map/all_to_all | solution.py:48
  171.3 1.5 copy-start.2
  171.3 1.5 copy-start.3
  172.7 9.3 %copy-start.1 = (f32[2,8,16,128]{3,1,2,0:T(8,128)}, f32[2,8,16,128]{3,1,2,0:T(8,128)S(1)}, u32[]{:S(2)}) copy-start(f32[2,8,16,128]{3,1,2,0:T(8,128)S(1)} %copy.29) | copy-start | bytes 393220
where the time goes:
time: 185 us; the launch traced here: 182 us
  blocking collectives  57.1 us (31%)
  local copies, waits for them, and re-layouts  41.3 us (22%)
  waiting for transfers between devices  39.5 us (21%)
  starting transfers between devices  32.6 us (18%)
  matrix products  6.94 us (4%)
  other arithmetic  3.83 us (2%)
    all_to_all x1, blocking collectives, local(): lax.all_to_all(packed.reshape(devices, capacity, band_count, patch_width)...  48.5 us
    all_to_all x1, waiting for transfers between devices, local(): lax.all_to_all(packed.reshape(devices, capacity, band_count, patch_width)...  39.5 us
    scatter x2, local copies, waits for them, and re-layouts, local(): packed = jnp.zeros((devices * capacity, band_count, patch_width), jnp.flo...  23.4 us
    all_to_all x1, starting transfers between devices, local(): lax.all_to_all(slot_tiles.reshape(devices, capacity), 'tiles', split_axis...  18.4 us
    all_to_all x1, starting transfers between devices, local(): lax.all_to_all(packed.reshape(devices, capacity, band_count, patch_width)...  14.1 us
    psum x1, blocking collectives, local(): emis_grad = lax.psum(partial_grad, 'bands') / BANDS  8.58 us
    reshape x2, local copies, waits for them, and re-layouts, local(): packed.reshape(devices, capacity, band_count, patch_width)  5.95 us
    dot_general x2, matrix products, local(): jnp.einsum('bkp,kpq->kbq', picked, view_tiles, preferred_element_type=jnp...  5.68 us
  transfers between devices with their start and end apart: 2, of which 1 were waited for; matrix products, arithmetic and copies ran while one was open for 14% of the time, Pallas kernels for 0%

commit v1 on v0

v1 whole, which is shorter than its diff:
```python
import functools

import jax
import jax.numpy as jnp
from jax import lax
from jax.experimental import pallas as pl
from jax.experimental.pallas import tpu as pltpu
from jax.sharding import PartitionSpec as P

BANDS = 48
ITERS = 2
PATCH = 128
CAP = 2
CORES = 2
PAIRS = 2
F32, BF16 = jnp.float32, jnp.bfloat16
MESH = pl.DeviceIdType.MESH


def far_first(n):
    out = []
    for d in range(n // 2, 0, -1):
        out.append(d)
        if n - d != d:
            out.append(n - d)
    return out


def kernel(dims, *refs):
    nz, ny, nx = dims
    (view_hbm, rows_ref, cols_ref, seed_ref, emis_ref, power_ref, irr_ref,
     adj_ref, grad_ref,
     view, scaled, terms, prev, pick, select, sum_rows, mid_rest, acc,
     meta_send, meta_recv, s1_send, s1_recv, s2_send, s2_recv, g_part, g_recv,
     view_sem, meta_ss, meta_rs, s1_ss, s1_rs, s2_ss, s2_rs, g_ss, g_rs) = refs
    nblk = view.shape[0]
    bands, width = seed_ref.shape
    tiles = width // PATCH
    bp = bands // PAIRS
    hb = bp // 2
    me = lax.axis_index("tiles")
    my_x = lax.axis_index("bands")
    my_c = lax.rem(me, CORES)
    my_y = lax.rem(me // CORES, ny)
    my_z = me // (CORES * ny)
    ring = (ny, nz)
    ring2 = (nz, ny)
    mine = (my_y, my_z)
    mine2 = (my_z, my_y)

    def index_of(kind, first, second, core):
        y, z = (first, second) if kind == 0 else (second, first)
        return (z * ny + y) * CORES + core

    peers1, peers2 = [], []
    for kind in (0, 1):
        p1, p2 = [], []
        for off in far_first(ring[kind]) + [0]:
            for dc in range(CORES):
                if off == 0 and dc == 0:
                    continue
                pos = lax.rem(mine[kind] + off, ring[kind])
                core = lax.rem(my_c + dc, CORES)
                p1.append((kind, pos, core, index_of(kind, pos, mine2[kind], core), off, dc))
        for off in far_first(ring2[kind]):
            pos = lax.rem(mine2[kind] + off, ring2[kind])
            p2.append((kind, pos, index_of(kind, mine[kind], pos, my_c)))
        peers1.append(p1)
        peers2.append(p2)

    def interleave(a, b):
        out = []
        for i in range(max(len(a), len(b))):
            out += a[i:i + 1] + b[i:i + 1]
        return out

    order1 = interleave(*peers1)
    order2 = interleave(*peers2)
    x_peers = [lax.rem(my_x + off, nx) for off in range(1, nx)]

    view_copy = pltpu.make_async_copy(view_hbm, view, view_sem)
    view_copy.start()
    barrier = pltpu.get_barrier_semaphore()
    met = 0
    for kind, pos, core, dev, off, dc in order1:
        if kind == 1 and off == 0:
            continue
        pl.semaphore_signal(barrier, inc=1, device_id={"tiles": dev}, device_id_type=MESH)
        met += 1
    for x in x_peers:
        pl.semaphore_signal(barrier, inc=1, device_id={"bands": x}, device_id_type=MESH)
        met += 1

    col_row = cols_ref[...]
    lane = lax.broadcasted_iota(jnp.int32, (nblk, nblk), 1)
    sub = lax.broadcasted_iota(jnp.int32, (nblk, nblk), 0)
    spread = jnp.broadcast_to(col_row, (nblk, nblk))
    col_col = jnp.sum(jnp.where(lane == sub, spread, 0).astype(F32), axis=1, keepdims=True).astype(jnp.int32)
    tgt_row = lax.shift_right_logical(spread, tiles.bit_length() - 1)
    tgt_col = lax.shift_right_logical(jnp.broadcast_to(col_col, (nblk, nblk)), tiles.bit_length() - 1)
    same = tgt_row == tgt_col
    rank_row = jnp.sum(jnp.where(same & (sub < lane), 1.0, 0.0), axis=0, keepdims=True).astype(jnp.int32)
    rank_col = jnp.sum(jnp.where(same & (lane < sub), 1.0, 0.0), axis=1, keepdims=True).astype(jnp.int32)
    tb = tiles.bit_length() - 1
    cb = CORES.bit_length() - 1
    yb = ny.bit_length() - 1

    def place(cols, rank, kind):
        tile = cols & (tiles - 1)
        core = lax.shift_right_logical(cols, tb) & (CORES - 1)
        y = lax.shift_right_logical(cols, tb + cb) & (ny - 1)
        z = lax.shift_right_logical(cols, tb + cb + yb)
        first, second = (y, z) if kind == 0 else (z, y)
        slots = ring2[kind] * CAP
        return (first * CORES + core) * slots + second * CAP + rank, second * tiles + tile

    for kind in (0, 1):
        n1 = ring[kind] * CORES
        slots = ring2[kind] * CAP
        pos_row, _ = place(col_row, rank_row, kind)
        pos_col, id_col = place(col_col, rank_col, kind)
        slot_no = lax.broadcasted_iota(jnp.int32, (n1 * slots, nblk), 0)
        pick[kind] = jnp.where(slot_no == pos_row, 1.0, 0.0).astype(BF16)
        lane_slot = lax.broadcasted_iota(jnp.int32, (nblk, PATCH), 1) & (slots - 1)
        id_value = (id_col + 1).astype(F32)
        pos_wide = jnp.broadcast_to(pos_col, (nblk, PATCH)) - lane_slot
        for q in range(n1):
            hit = jnp.where(pos_wide == q * slots, id_value, 0.0)
            meta_send[kind, q] = jnp.sum(hit, axis=0, keepdims=True) - 1.0

    def scale(p, first):
        lo = p * bp
        for t in range(tiles):
            lanes = slice(t * PATCH, (t + 1) * PATCH)
            adj = seed_ref[lo:lo + bp, lanes]
            if not first:
                adj = adj + acc[p, pl.ds(t, bp, stride=tiles), :]
            scaled[p, t, 0:bp, :] = ((1.0 - emis_ref[0:1, lanes]) * adj).astype(BF16)

    def products(p):
        group = 24

        def body(step, carry):
            base = step * group
            for j in range(0, group, 2):
                k = base + j
                r0 = rows_ref[k] & (tiles - 1)
                r1 = rows_ref[k + 1] & (tiles - 1)
                left = jnp.concatenate([scaled[p, r0], scaled[p, r1]], axis=0)
                right = jnp.concatenate([view[k], view[k + 1]], axis=1)
                out = jnp.dot(left, right, preferred_element_type=F32)
                n = scaled.shape[2]
                terms[p, pl.ds(k, bp, stride=nblk), :] = out[0:bp, 0:PATCH]
                terms[p, pl.ds(k + 1, bp, stride=nblk), :] = out[n:n + bp, PATCH:2 * PATCH]
            return carry

        lax.fori_loop(0, nblk // group, body, 0)

    def choose(it, p):
        for j in range(bp):
            kind, jb = divmod(j, hb)
            rows = slice(j * nblk, (j + 1) * nblk)
            value = terms[p, rows, :]
            if it == 0:
                value = value.astype(BF16)
                prev[p, rows, :] = value
            else:
                value = (value - prev[p, rows, :].astype(F32)).astype(BF16)
            n1 = ring[kind] * CORES
            slots = ring2[kind] * CAP
            out = jnp.dot(pick[kind], value, preferred_element_type=F32).astype(BF16)
            s1_send[it, p, kind, :, jb] = out.reshape(n1, slots, PATCH)
        for kind in (0, 1):
            own = mine[kind] * CORES + my_c
            s1_recv[it, p, kind, own] = s1_send[it, p, kind, own]

    def send1(it, p):
        for kind, pos, core, dev, off, dc in order1:
            pltpu.make_async_remote_copy(
                src_ref=s1_send.at[it, p, kind, pos * CORES + core],
                dst_ref=s1_recv.at[it, p, kind, mine[kind] * CORES + my_c],
                send_sem=s1_ss.at[it, p, kind], recv_sem=s1_rs.at[it, p, kind],
                device_id={"tiles": dev}, device_id_type=MESH).start()

    def wait1(it, p, kind):
        n1 = ring[kind] * CORES
        ref = s1_recv.at[it, p, kind, 0:n1 - 1]
        pltpu.make_async_copy(ref, ref, s1_rs.at[it, p, kind]).wait()

    def send_meta():
        for kind, pos, core, dev, off, dc in order1:
            pltpu.make_async_remote_copy(
                src_ref=meta_send.at[kind, pos * CORES + core],
                dst_ref=meta_recv.at[kind, mine[kind] * CORES + my_c],
                send_sem=meta_ss.at[kind], recv_sem=meta_rs.at[kind],
                device_id={"tiles": dev}, device_id_type=MESH).start()

    def take_meta(kind):
        n1 = ring[kind] * CORES
        slots = ring2[kind] * CAP
        own = mine[kind] * CORES + my_c
        ref = meta_recv.at[kind, 0:n1 - 1]
        pltpu.make_async_copy(ref, ref, meta_rs.at[kind]).wait()
        meta_recv[kind, own] = meta_send[kind, own]
        per = PATCH // slots
        rows = ring2[kind] * tiles
        part = lax.broadcasted_iota(jnp.int32, (1, PATCH), 1) // slots
        row_no = lax.broadcasted_iota(jnp.int32, (rows, PATCH), 0).astype(F32)
        for h in range(n1 // per):
            ids = jnp.zeros((1, PATCH), F32)
            for j in range(per):
                ids = jnp.where(part == j, meta_recv[kind, h * per + j], ids)
            select[kind, :, h * PATCH:(h + 1) * PATCH] = jnp.where(row_no == ids, 1.0, 0.0).astype(BF16)

    def middle(it, p, kind):
        n1 = ring[kind] * CORES
        n2 = ring2[kind]
        slots = n2 * CAP
        for jb in range(hb):
            got = s1_recv[it, p, kind, :, jb].reshape(n1 * slots, PATCH)
            total = jnp.dot(select[kind], got, preferred_element_type=F32)
            if it > 0:
                total = total + mid_rest[p, kind, jb]
            out = total.astype(BF16)
            if it < ITERS - 1:
                mid_rest[p, kind, jb] = total - out.astype(F32)
            s2_send[it, p, kind, :, jb] = out.reshape(n2, tiles, PATCH)
        own = mine2[kind]
        s2_recv[it, p, kind, own] = s2_send[it, p, kind, own]

    def send2(it, p, kinds):
        for kind, pos, dev in order2:
            if kind in kinds:
                pltpu.make_async_remote_copy(
                    src_ref=s2_send.at[it, p, kind, pos],
                    dst_ref=s2_recv.at[it, p, kind, mine2[kind]],
                    send_sem=s2_ss.at[it, p, kind], recv_sem=s2_rs.at[it, p, kind],
                    device_id={"tiles": dev}, device_id_type=MESH).start()

    def finish(it, p):
        for kind in (0, 1):
            n2 = ring2[kind]
            ref = s2_recv.at[it, p, kind, 0:n2 - 1]
            pltpu.make_async_copy(ref, ref, s2_rs.at[it, p, kind]).wait()
            for jb in range(hb):
                total = s2_recv[it, p, kind, 0, jb].astype(F32)
                for j in range(1, n2):
                    total = total + s2_recv[it, p, kind, j, jb].astype(F32)
                row = (kind * hb + jb) * tiles
                if it > 0:
                    total = total + acc[p, row:row + tiles, :]
                acc[p, row:row + tiles, :] = total

    if scaled.shape[2] > bp:
        pad = scaled.shape[2] - bp
        for p in range(PAIRS):
            scaled[p, :, bp:, :] = jnp.zeros((tiles, pad, PATCH), BF16)
    for p in range(PAIRS):
        scale(p, True)
    view_copy.wait()
    for it in range(ITERS):
        for p in range(PAIRS):
            if it > 0:
                finish(it - 1, p)
                scale(p, False)
            products(p)
            choose(it, p)
            if it == 0 and p == 0:
                pl.semaphore_wait(barrier, met)
            send1(it, p)
            if it == 0 and p == 0:
                send_meta()
        for p in range(PAIRS):
            if it == 0 and p == 0:
                take_meta(0)
                take_meta(1)
            for kind in (0, 1):
                wait1(it, p, kind)
                middle(it, p, kind)
                send2(it, p, (kind,))

    for p in range(PAIRS):
        finish(ITERS - 1, p)
        lo = p * bp
        for t in range(tiles):
            lanes = slice(t * PATCH, (t + 1) * PATCH)
            adj = seed_ref[lo:lo + bp, lanes] + acc[p, pl.ds(t, bp, stride=tiles), :]
            adj_ref[lo:lo + bp, lanes] = adj
            contrast = power_ref[lo:lo + bp, lanes] - irr_ref[lo:lo + bp, lanes]
            part = jnp.sum(adj * contrast, axis=0, keepdims=True)
            if p > 0:
                part = part + g_part[t:t + 1, :]
            g_part[t:t + 1, :] = part
    for i, x in enumerate(x_peers):
        pltpu.make_async_remote_copy(
            src_ref=g_part, dst_ref=g_recv.at[i], send_sem=g_ss, recv_sem=g_rs,
            device_id={"bands": x}, device_id_type=MESH).start()
    for kind in (0, 1):
        n1 = ring[kind] * CORES
        n2 = ring2[kind]
        ref = meta_send.at[kind, 0:n1 - 1]
        pltpu.make_async_copy(ref, ref, meta_ss.at[kind]).wait()
        for it in range(ITERS):
            for p in range(PAIRS):
                ref = s1_send.at[it, p, kind, 0:n1 - 1]
                pltpu.make_async_copy(ref, ref, s1_ss.at[it, p, kind]).wait()
                ref = s2_send.at[it, p, kind, 0:n2 - 1]
                pltpu.make_async_copy(ref, ref, s2_ss.at[it, p, kind]).wait()
    pltpu.make_async_copy(g_recv, g_recv, g_rs).wait()
    total = g_part[...]
    for i in range(nx - 1):
        total = total + g_recv[i]
    grad_ref[...] = total * (1.0 / BANDS)
    pltpu.make_async_copy(g_recv, g_recv, g_ss).wait()


def local(dims, view_tiles, vis_rows, vis_cols, seed_grad, emissivity, emissive_power, irradiance):
    nz, ny, nx = dims
    nblk = view_tiles.shape[0]
    bands, width = seed_grad.shape
    tiles = width // PATCH
    bp = bands // PAIRS
    hb = bp // 2
    rp = -(-bp // 8) * 8
    n1, n2 = ny * CORES, nz
    slots = n2 * CAP
    vmem = pl.BlockSpec(memory_space=pltpu.VMEM)
    dma = pltpu.SemaphoreType.DMA
    adjoint, grad = pl.pallas_call(
        functools.partial(kernel, dims),
        out_shape=(jax.ShapeDtypeStruct((bands, width), F32), jax.ShapeDtypeStruct((tiles, PATCH), F32)),
        in_specs=[pl.BlockSpec(memory_space=pl.ANY), pl.BlockSpec(memory_space=pltpu.SMEM)] + [vmem] * 5,
        out_specs=(vmem, vmem),
        scratch_shapes=[
            pltpu.VMEM((nblk, PATCH, PATCH), BF16),
            pltpu.VMEM((PAIRS, tiles, rp, PATCH), BF16),
            pltpu.VMEM((PAIRS, bp * nblk, PATCH), F32),
            pltpu.VMEM((PAIRS, bp * nblk, PATCH), BF16),
            pltpu.VMEM((2, n1 * slots, nblk), BF16),
            pltpu.VMEM((2, n2 * tiles, n1 * slots), BF16),
            pltpu.VMEM((8, PATCH), F32),
            pltpu.VMEM((PAIRS, 2, hb, n2 * tiles, PATCH), F32),
            pltpu.VMEM((PAIRS, bp * tiles, PATCH), F32),
            pltpu.VMEM((2, n1, 1, PATCH), F32),
            pltpu.VMEM((2, n1, 1, PATCH), F32),
            pltpu.VMEM((ITERS, PAIRS, 2, n1, hb, slots, PATCH), BF16),
            pltpu.VMEM((ITERS, PAIRS, 2, n1, hb, slots, PATCH), BF16),
            pltpu.VMEM((ITERS, PAIRS, 2, n2, hb, tiles, PATCH), BF16),
            pltpu.VMEM((ITERS, PAIRS, 2, n2, hb, tiles, PATCH), BF16),
            pltpu.VMEM((tiles, PATCH), F32),
            pltpu.VMEM((nx - 1, tiles, PATCH), F32),
            dma,
            dma((2,)), dma((2,)),
            dma((ITERS, PAIRS, 2)), dma((ITERS, PAIRS, 2)),
            dma((ITERS, PAIRS, 2)), dma((ITERS, PAIRS, 2)),
            dma, dma,
        ],
        compiler_params=pltpu.CompilerParams(
            collective_id=0, has_side_effects=True, vmem_limit_bytes=40 * 2**20),
    )(view_tiles, vis_rows, vis_cols.reshape(1, nblk), seed_grad, emissivity.reshape(1, width),
      emissive_power, irradiance)
    return adjoint, grad.reshape(width)


def solution(mesh):
    placed = (
        P("tiles", None, None),
        P("tiles"),
        P("tiles"),
        P("bands", "tiles"),
        P("tiles"),
        P("bands", "tiles"),
        P("bands", "tiles"),
    )
    side = 1
    while side * side * CORES < mesh.shape["tiles"]:
        side *= 2
    dims = (mesh.shape["tiles"] // (CORES * side), side, mesh.shape["bands"])
    return jax.shard_map(
        functools.partial(local, dims),
        mesh=mesh,
        in_specs=placed,
        out_specs=(P("bands", "tiles"), P("tiles")),
        check_vma=False,
    )
```

time: 185 us -> 59.9 us (0.32); the launches traced: 182 us -> 59.6 us
  blocking collectives: 57.1 us -> 0 us
  Pallas kernels: 0 us -> 51.1 us
  waiting for transfers between devices: 39.5 us -> 0 us
  local copies, waits for them, and re-layouts: 41.3 us -> 7.86 us
  starting transfers between devices: 32.6 us -> 0 us
  matrix products: 6.94 us -> 0 us
  other arithmetic: 3.83 us -> 0 us
    pallas_call x0 -> x1, Pallas kernels: none -> 51.1 us  [local(): pl.pallas_call(functools.partial(kernel, dims), out_shape=(jax.ShapeDtype...]
    all_to_all x1 -> x0, blocking collectives: 48.5 us -> none  [local(): lax.all_to_all(packed.reshape(devices, capacity, band_count, patch_width)...]
    all_to_all x2 -> x0, waiting for transfers between devices: 39.5 us -> none  [the longest x1 39.5 us: local(): lax.all_to_all(packed.reshape(devices, capacity, band_count, patch_width)...]
    all_to_all x2 -> x0, starting transfers between devices: 32.6 us -> none  [the longest x1 18.4 us: local(): lax.all_to_all(slot_tiles.reshape(devices, capacity), 'tiles', split_axis...]
    scatter x3 -> x0, local copies, waits for them, and re-layouts: 24.2 us -> none  [the longest x2 23.4 us: local(): packed = jnp.zeros((devices * capacity, band_count, patch_width), jnp.flo...]
    psum x1 -> x0, blocking collectives: 8.58 us -> none  [local(): emis_grad = lax.psum(partial_grad, 'bands') / BANDS]
    dot_general x4 -> x0, matrix products: 6.94 us -> none  [the longest x2 5.68 us: local(): jnp.einsum('bkp,kpq->kbq', picked, view_tiles, preferred_element_type=jnp...]
    unnamed x11 -> x16, local copies, waits for them, and re-layouts: 1.01 us -> 7.86 us
  transfers between devices with their start and end apart: 2 -> 0, of which waited for: 1 -> 0; matrix products, arithmetic and copies ran while one was open for 14% -> 0% of each run, Pallas kernels for 0% -> 0%
where the time goes in v1:
time: 59.9 us; the launch traced here: 59.6 us
  Pallas kernels  51.1 us (85%)
  local copies, waits for them, and re-layouts  7.86 us (13%)
  between operations  0.66 us (1%)
    pallas_call x1, Pallas kernels, local(): pl.pallas_call(functools.partial(kernel, dims), out_shape=(jax.ShapeDtype...  51.1 us
    unnamed x16, local copies, waits for them, and re-layouts  7.86 us

profile of v1, /device:TPU:1, one launch (start us, length us, event | category | flops | bytes accessed | tf_op | source)
XLA Modules:
  0.0 59.6 jit_solution(8890167717549709068)
XLA Ops:
  0.6 0.0 copy-start
  0.6 1.9 %copy-done = bf16[96,128,128]{2,1,0:T(8,128)(2,1)S(1)} copy-done((bf16[96,128,128]{2,1,0:T(8,128)(2,1)S(1)}, bf16[96,128,128]{2,1,0:T(8,128)(2,1)}, u32[]{:S(2)}) %copy-start) | copy-done | bytes 3145752
  2.5 0.0 copy-start.1
  2.5 0.9 %copy-done.1 = f32[12,2048]{1,0:T(8,128)S(1)} copy-done((f32[12,2048]{1,0:T(8,128)S(1)}, f32[12,2048]{1,0:T(8,128)}, u32[]{:S(2)}) %copy-start.1) | copy-done | bytes 98328
  3.4 0.0 copy-start.2
  3.4 0.9 %copy-done.2 = f32[12,2048]{1,0:T(8,128)S(1)} copy-done((f32[12,2048]{1,0:T(8,128)S(1)}, f32[12,2048]{1,0:T(8,128)}, u32[]{:S(2)}) %copy-start.2) | copy-done | bytes 98328
  4.3 0.0 copy-start.3
  4.3 0.9 %copy-done.3 = f32[12,2048]{1,0:T(8,128)S(1)} copy-done((f32[12,2048]{1,0:T(8,128)S(1)}, f32[12,2048]{1,0:T(8,128)}, u32[]{:S(2)}) %copy-start.3) | copy-done | bytes 98328
  5.2 0.0 copy-start.4
  5.2 0.7 %copy-done.4 = f32[2048]{0:T(1024)S(1)} copy-done((f32[2048]{0:T(1024)S(1)}, f32[2048]{0:T(1024)}, u32[]{:S(2)}) %copy-start.4) | copy-done | bytes 8216
  5.9 0.0 copy-start.5
  5.9 0.7 %copy-done.5 = s32[96]{0:T(128)S(1)} copy-done((s32[96]{0:T(128)S(1)}, s32[96]{0:T(128)}, u32[]{:S(2)}) %copy-start.5) | copy-done | bytes 408
  6.6 0.0 copy-start.6
  6.6 0.7 %copy-done.6 = s32[96]{0:T(128)S(1)} copy-done((s32[96]{0:T(128)S(1)}, s32[96]{0:T(128)}, u32[]{:S(2)}) %copy-start.6) | copy-done | bytes 408
  7.2 51.1 %shard_map.86 = (f32[12,2048]{1,0:T(8,128)S(1)}, f32[16,128]{1,0:T(8,128)S(1)}) custom-call(bf16[96,128,128]{2,1,0:T(8,128)(2,1)S(1)} %copy-done, s32[96]{0:T(128)S(1)} %copy-done.5, s32[1,96]{1,0:T(1,128)S(1)} %bitcast.5, f32[12,2048]{1,0:T(8,128)S(1)} %copy-done.1, f32[1,2048]{1,0:T(1,128)S(1)} %bitcast.3, f32[12,2048]{1,0:T(8,128)S(1)} %copy-done.2, ...), custom_call_target="tpu_custom_call" | custom-call | tf_op jit(solution)/shard_map/pallas_call | solution.py:329
  58.4 0.7 %copy.11 = f32[12,2048]{1,0:T(8,128)} copy(f32[12,2048]{1,0:T(8,128)S(1)} %get-tuple-element.8) | data formatting | bytes 196608
  59.0 0.6 %copy.12 = f32[2048]{0:T(1024)} copy(f32[2048]{0:T(1024)S(1)} %bitcast.4) | data formatting | bytes 16384
Async XLA Ops:
  0.6 1.9 %copy-start = (bf16[96,128,128]{2,1,0:T(8,128)(2,1)S(1)}, bf16[96,128,128]{2,1,0:T(8,128)(2,1)}, u32[]{:S(2)}) copy-start(bf16[96,128,128]{2,1,0:T(8,128)(2,1)} %refs_0_.1) | copy-start | bytes 9437188
  2.5 0.9 %copy-start.1 = (f32[12,2048]{1,0:T(8,128)S(1)}, f32[12,2048]{1,0:T(8,128)}, u32[]{:S(2)}) copy-start(f32[12,2048]{1,0:T(8,128)} %refs_3_.1) | copy-start | bytes 294916
  3.4 0.9 %copy-start.2 = (f32[12,2048]{1,0:T(8,128)S(1)}, f32[12,2048]{1,0:T(8,128)}, u32[]{:S(2)}) copy-start(f32[12,2048]{1,0:T(8,128)} %refs_5_.1) | copy-start | bytes 294916
  4.3 0.9 %copy-start.3 = (f32[12,2048]{1,0:T(8,128)S(1)}, f32[12,2048]{1,0:T(8,128)}, u32[]{:S(2)}) copy-start(f32[12,2048]{1,0:T(8,128)} %refs_6_.1) | copy-start | bytes 294916
  5.2 0.7 %copy-start.4 = (f32[2048]{0:T(1024)S(1)}, f32[2048]{0:T(1024)}, u32[]{:S(2)}) copy-start(f32[2048]{0:T(1024)} %param.11) | copy-start | bytes 24580
  5.9 0.7 %copy-start.5 = (s32[96]{0:T(128)S(1)}, s32[96]{0:T(128)}, u32[]{:S(2)}) copy-start(s32[96]{0:T(128)} %refs_1_.1) | copy-start | bytes 1156
  6.6 0.7 %copy-start.6 = (s32[96]{0:T(128)S(1)}, s32[96]{0:T(128)}, u32[]{:S(2)}) copy-start(s32[96]{0:T(128)} %param.9) | copy-start | bytes 1156

commit v2 on v1

--- a/solution.py
+++ b/solution.py
@@ -12,7 +12,8 @@
 PATCH = 128
 CAP = 2
 CORES = 2
-PAIRS = 2
+PAIRS = 3
+GROUP = 24
 F32, BF16 = jnp.float32, jnp.bfloat16
 MESH = pl.DeviceIdType.MESH
 
@@ -28,11 +29,12 @@
 
 def kernel(dims, *refs):
     nz, ny, nx = dims
-    (view_hbm, rows_ref, cols_ref, seed_ref, emis_ref, power_ref, irr_ref,
+    (view_hbm, rows_hbm, cols_hbm, seed_hbm, emis_hbm, power_hbm, irr_hbm,
      adj_ref, grad_ref,
-     view, scaled, terms, prev, pick, select, sum_rows, mid_rest, acc,
+     view, rows_ref, cols_ref, seed_ref, emis_ref, power_ref, irr_ref,
+     scaled, terms, prev, pick, select, mid_rest, acc,
      meta_send, meta_recv, s1_send, s1_recv, s2_send, s2_recv, g_part, g_recv,
-     view_sem, meta_ss, meta_rs, s1_ss, s1_rs, s2_ss, s2_rs, g_ss, g_rs) = refs
+     in_sems, view_sems, meta_ss, meta_rs, s1_ss, s1_rs, s2_ss, s2_rs, g_ss, g_rs) = refs
     nblk = view.shape[0]
     bands, width = seed_ref.shape
     tiles = width // PATCH
@@ -78,8 +80,21 @@
     order2 = interleave(*peers2)
     x_peers = [lax.rem(my_x + off, nx) for off in range(1, nx)]
 
-    view_copy = pltpu.make_async_copy(view_hbm, view, view_sem)
-    view_copy.start()
+    cols_in, rows_in, seed_in, emis_in, power_in, irr_in = [
+        pltpu.make_async_copy(src, dst, in_sems.at[i]) for i, (src, dst) in enumerate((
+            (cols_hbm, cols_ref), (rows_hbm, rows_ref), (seed_hbm, seed_ref), (emis_hbm, emis_ref),
+            (power_hbm, power_ref), (irr_hbm, irr_ref)))]
+
+    def view_in(step):
+        part = pl.ds(step * GROUP, GROUP)
+        return pltpu.make_async_copy(view_hbm.at[part], view.at[part], view_sems.at[step])
+
+    for copy in (cols_in, rows_in, seed_in, emis_in):
+        copy.start()
+    for step in range(nblk // GROUP):
+        view_in(step).start()
+    power_in.start()
+    irr_in.start()
     barrier = pltpu.get_barrier_semaphore()
     met = 0
     for kind, pos, core, dev, off, dc in order1:
@@ -91,6 +106,7 @@
         pl.semaphore_signal(barrier, inc=1, device_id={"bands": x}, device_id_type=MESH)
         met += 1
 
+    cols_in.wait()
     col_row = cols_ref[...]
     lane = lax.broadcasted_iota(jnp.int32, (nblk, nblk), 1)
     sub = lax.broadcasted_iota(jnp.int32, (nblk, nblk), 0)
@@ -137,12 +153,12 @@
                 adj = adj + acc[p, pl.ds(t, bp, stride=tiles), :]
             scaled[p, t, 0:bp, :] = ((1.0 - emis_ref[0:1, lanes]) * adj).astype(BF16)
 
-    def products(p):
-        group = 24
-
+    def products(p, arriving):
         def body(step, carry):
-            base = step * group
-            for j in range(0, group, 2):
+            base = step * GROUP
+            if arriving:
+                view_in(step).wait()
+            for j in range(0, GROUP, 2):
                 k = base + j
                 r0 = rows_ref[k] & (tiles - 1)
                 r1 = rows_ref[k + 1] & (tiles - 1)
@@ -154,7 +170,7 @@
                 terms[p, pl.ds(k + 1, bp, stride=nblk), :] = out[n:n + bp, PATCH:2 * PATCH]
             return carry
 
-        lax.fori_loop(0, nblk // group, body, 0)
+        lax.fori_loop(0, nblk // GROUP, body, 0)
 
     def choose(it, p):
         for j in range(bp):
@@ -255,15 +271,15 @@
         pad = scaled.shape[2] - bp
         for p in range(PAIRS):
             scaled[p, :, bp:, :] = jnp.zeros((tiles, pad, PATCH), BF16)
-    for p in range(PAIRS):
-        scale(p, True)
-    view_copy.wait()
+    seed_in.wait()
+    emis_in.wait()
+    rows_in.wait()
     for it in range(ITERS):
         for p in range(PAIRS):
             if it > 0:
                 finish(it - 1, p)
-                scale(p, False)
-            products(p)
+            scale(p, it == 0)
+            products(p, it == 0 and p == 0)
             choose(it, p)
             if it == 0 and p == 0:
                 pl.semaphore_wait(barrier, met)
@@ -279,6 +295,8 @@
                 middle(it, p, kind)
                 send2(it, p, (kind,))
 
+    power_in.wait()
+    irr_in.wait()
     for p in range(PAIRS):
         finish(ITERS - 1, p)
         lo = p * bp
@@ -314,6 +332,15 @@
     pltpu.make_async_copy(g_recv, g_recv, g_ss).wait()
 
 
+def hand_on(adj_ref, grad_ref, adj_out, grad_out, sems):
+    copies = [pltpu.make_async_copy(adj_ref, adj_out, sems.at[0]),
+              pltpu.make_async_copy(grad_ref, grad_out, sems.at[1])]
+    for copy in copies:
+        copy.start()
+    for copy in copies:
+        copy.wait()
+
+
 def local(dims, view_tiles, vis_rows, vis_cols, seed_grad, emissivity, emissive_power, irradiance):
     nz, ny, nx = dims
     nblk = view_tiles.shape[0]
@@ -324,21 +351,28 @@
     rp = -(-bp // 8) * 8
     n1, n2 = ny * CORES, nz
     slots = n2 * CAP
+    hbm = pl.BlockSpec(memory_space=pltpu.HBM)
     vmem = pl.BlockSpec(memory_space=pltpu.VMEM)
     dma = pltpu.SemaphoreType.DMA
-    adjoint, grad = pl.pallas_call(
+    shapes = (jax.ShapeDtypeStruct((bands, width), F32), jax.ShapeDtypeStruct((tiles, PATCH), F32))
+    results = pl.pallas_call(
         functools.partial(kernel, dims),
-        out_shape=(jax.ShapeDtypeStruct((bands, width), F32), jax.ShapeDtypeStruct((tiles, PATCH), F32)),
-        in_specs=[pl.BlockSpec(memory_space=pl.ANY), pl.BlockSpec(memory_space=pltpu.SMEM)] + [vmem] * 5,
+        out_shape=shapes,
+        in_specs=[hbm] * 7,
         out_specs=(vmem, vmem),
         scratch_shapes=[
             pltpu.VMEM((nblk, PATCH, PATCH), BF16),
+            pltpu.SMEM((nblk,), jnp.int32),
+            pltpu.VMEM((1, nblk), jnp.int32),
+            pltpu.VMEM((bands, width), F32),
+            pltpu.VMEM((1, width), F32),
+            pltpu.VMEM((bands, width), F32),
+            pltpu.VMEM((bands, width), F32),
             pltpu.VMEM((PAIRS, tiles, rp, PATCH), BF16),
             pltpu.VMEM((PAIRS, bp * nblk, PATCH), F32),
             pltpu.VMEM((PAIRS, bp * nblk, PATCH), BF16),
             pltpu.VMEM((2, n1 * slots, nblk), BF16),
             pltpu.VMEM((2, n2 * tiles, n1 * slots), BF16),
-            pltpu.VMEM((8, PATCH), F32),
             pltpu.VMEM((PAIRS, 2, hb, n2 * tiles, PATCH), F32),
             pltpu.VMEM((PAIRS, bp * tiles, PATCH), F32),
             pltpu.VMEM((2, n1, 1, PATCH), F32),
@@ -349,7 +383,7 @@
             pltpu.VMEM((ITERS, PAIRS, 2, n2, hb, tiles, PATCH), BF16),
             pltpu.VMEM((tiles, PATCH), F32),
             pltpu.VMEM((nx - 1, tiles, PATCH), F32),
-            dma,
+            dma((6,)), dma((nblk // GROUP,)),
             dma((2,)), dma((2,)),
             dma((ITERS, PAIRS, 2)), dma((ITERS, PAIRS, 2)),
             dma((ITERS, PAIRS, 2)), dma((ITERS, PAIRS, 2)),
@@ -357,8 +391,10 @@
         ],
         compiler_params=pltpu.CompilerParams(
             collective_id=0, has_side_effects=True, vmem_limit_bytes=40 * 2**20),
-    )(view_tiles, vis_rows, vis_cols.reshape(1, nblk), seed_grad, emissivity.reshape(1, width),
-      emissive_power, irradiance)
+    )(*[pltpu.with_memory_space_constraint(x, pltpu.HBM) for x in (
+        view_tiles, vis_rows, vis_cols.reshape(1, nblk), seed_grad, emissivity.reshape(1, width),
+        emissive_power, irradiance)])
+    adjoint, grad = results
     return adjoint, grad.reshape(width)
 
 

time: 59.9 us -> 51.6 us (0.86)
  local copies, waits for them, and re-layouts: 7.86 us -> 1.26 us
  Pallas kernels: 51.1 us -> 49.6 us
    unnamed x16 -> x2, local copies, waits for them, and re-layouts: 7.86 us -> 1.26 us
    pallas_call x1, Pallas kernels: 51.1 us -> 49.6 us  [local(): pl.pallas_call(functools.partial(kernel, dims), out_shape=shapes, in_spec...]
where the time goes in v2:
time: 51.6 us; the launch traced here: 51.5 us
  Pallas kernels  49.6 us (96%)
  local copies, waits for them, and re-layouts  1.26 us (2%)
  between operations  0.64 us (1%)
    pallas_call x1, Pallas kernels, local(): pl.pallas_call(functools.partial(kernel, dims), out_shape=shapes, in_spec...  49.6 us
    unnamed x2, local copies, waits for them, and re-layouts  1.26 us

profile of v2, /device:TPU:1, one launch (start us, length us, event | category | flops | bytes accessed | tf_op | source)
XLA Modules:
  0.0 51.5 jit_solution(16990978839044810018)
XLA Ops:
  0.6 49.6 %shard_map.86 = (f32[12,2048]{1,0:T(8,128)S(1)}, f32[16,128]{1,0:T(8,128)S(1)}) custom-call(bf16[96,128,128]{2,1,0:T(8,128)(2,1)} %refs_0_.1, s32[96]{0:T(128)} %refs_1_.1, s32[1,96]{1,0:T(1,128)} %bitcast.5, f32[12,2048]{1,0:T(8,128)} %refs_3_.1, f32[1,2048]{1,0:T(1,128)} %bitcast.4, f32[12,2048]{1,0:T(8,128)} %refs_5_.1, f32[12,2048]{1,0:T(8,128)} %refs_6_.1), custom_call_target="tpu_custom_call" | custom-call | tf_op jit(solution)/shard_map/pallas_call | solution.py:358
  50.2 0.7 %copy.11 = f32[12,2048]{1,0:T(8,128)} copy(f32[12,2048]{1,0:T(8,128)S(1)} %get-tuple-element.8) | data formatting | bytes 196608
  50.9 0.6 %copy.12 = f32[2048]{0:T(1024)} copy(f32[2048]{0:T(1024)S(1)} %bitcast.3) | data formatting | bytes 16384

commit v3 on v2

--- a/solution.py
+++ b/solution.py
@@ -15,6 +15,7 @@
 PAIRS = 3
 GROUP = 24
 F32, BF16 = jnp.float32, jnp.bfloat16
+ORDER = (("s", 0), ("s", 1), ("s", 2), ("m", 0), ("m", 1), ("m", 2), ("s", 3), ("s", 4), ("s", 5), ("m", 3), ("m", 4), ("m", 5))
 MESH = pl.DeviceIdType.MESH
 
 
@@ -58,7 +59,7 @@
     for kind in (0, 1):
         p1, p2 = [], []
         for off in far_first(ring[kind]) + [0]:
-            for dc in range(CORES):
+            for dc in (1, 0):
                 if off == 0 and dc == 0:
                     continue
                 pos = lax.rem(mine[kind] + off, ring[kind])
@@ -130,6 +131,7 @@
         slots = ring2[kind] * CAP
         return (first * CORES + core) * slots + second * CAP + rank, second * tiles + tile
 
+    placed = []
     for kind in (0, 1):
         n1 = ring[kind] * CORES
         slots = ring2[kind] * CAP
@@ -137,12 +139,7 @@
         pos_col, id_col = place(col_col, rank_col, kind)
         slot_no = lax.broadcasted_iota(jnp.int32, (n1 * slots, nblk), 0)
         pick[kind] = jnp.where(slot_no == pos_row, 1.0, 0.0).astype(BF16)
-        lane_slot = lax.broadcasted_iota(jnp.int32, (nblk, PATCH), 1) & (slots - 1)
-        id_value = (id_col + 1).astype(F32)
-        pos_wide = jnp.broadcast_to(pos_col, (nblk, PATCH)) - lane_slot
-        for q in range(n1):
-            hit = jnp.where(pos_wide == q * slots, id_value, 0.0)
-            meta_send[kind, q] = jnp.sum(hit, axis=0, keepdims=True) - 1.0
+        placed.append((pos_col, id_col))
 
     def scale(p, first):
         lo = p * bp
@@ -204,6 +201,15 @@
         pltpu.make_async_copy(ref, ref, s1_rs.at[it, p, kind]).wait()
 
     def send_meta():
+        for kind, (pos_col, id_col) in enumerate(placed):
+            n1 = ring[kind] * CORES
+            slots = ring2[kind] * CAP
+            lane_slot = lax.broadcasted_iota(jnp.int32, (nblk, PATCH), 1) & (slots - 1)
+            id_value = (id_col + 1).astype(F32)
+            pos_wide = jnp.broadcast_to(pos_col, (nblk, PATCH)) - lane_slot
+            for q in range(n1):
+                hit = jnp.where(pos_wide == q * slots, id_value, 0.0)
+                meta_send[kind, q] = jnp.sum(hit, axis=0, keepdims=True) - 1.0
         for kind, pos, core, dev, off, dc in order1:
             pltpu.make_async_remote_copy(
                 src_ref=meta_send.at[kind, pos * CORES + core],
@@ -274,26 +280,29 @@
     seed_in.wait()
     emis_in.wait()
     rows_in.wait()
-    for it in range(ITERS):
-        for p in range(PAIRS):
-            if it > 0:
-                finish(it - 1, p)
-            scale(p, it == 0)
-            products(p, it == 0 and p == 0)
-            choose(it, p)
-            if it == 0 and p == 0:
-                pl.semaphore_wait(barrier, met)
-            send1(it, p)
-            if it == 0 and p == 0:
-                send_meta()
-        for p in range(PAIRS):
-            if it == 0 and p == 0:
-                take_meta(0)
-                take_meta(1)
-            for kind in (0, 1):
-                wait1(it, p, kind)
-                middle(it, p, kind)
-                send2(it, p, (kind,))
+    def sweep(it, p):
+        if it > 0:
+            finish(it - 1, p)
+        scale(p, it == 0)
+        products(p, it == 0 and p == 0)
+        choose(it, p)
+        if it == 0 and p == 0:
+            pl.semaphore_wait(barrier, met)
+        send1(it, p)
+        if it == 0 and p == 0:
+            send_meta()
+
+    def turn(it, p):
+        if it == 0 and p == 0:
+            take_meta(0)
+            take_meta(1)
+        for kind in (0, 1):
+            wait1(it, p, kind)
+            middle(it, p, kind)
+            send2(it, p, (kind,))
+
+    for what, step in ORDER:
+        (sweep if what == "s" else turn)(*divmod(step, PAIRS))
 
     power_in.wait()
     irr_in.wait()
@@ -394,7 +403,13 @@
     )(*[pltpu.with_memory_space_constraint(x, pltpu.HBM) for x in (
         view_tiles, vis_rows, vis_cols.reshape(1, nblk), seed_grad, emissivity.reshape(1, width),
         emissive_power, irradiance)])
-    adjoint, grad = results
+    adjoint, grad = pl.pallas_call(
+        hand_on,
+        out_shape=shapes,
+        in_specs=[vmem] * 2,
+        out_specs=(hbm, hbm),
+        scratch_shapes=[dma((2,))],
+    )(*[pltpu.with_memory_space_constraint(x, pltpu.VMEM) for x in results])
     return adjoint, grad.reshape(width)
 
 

time: 51.6 us -> 50.8 us (0.984)
  local copies, waits for them, and re-layouts: 1.26 us -> 0 us
    unnamed x2 -> x0, local copies, waits for them, and re-layouts: 1.26 us -> none
    pallas_call x0 -> x1, Pallas kernels: none -> 0.68 us  [local(): pl.pallas_call(hand_on, out_shape=shapes, in_specs=[vmem] * 2, out_specs=...]
where the time goes in v3:
time: 50.8 us; the launch traced here: 50.5 us
  Pallas kernels  49.9 us (98%)
  between operations  0.64 us (1%)
    pallas_call x1, Pallas kernels, local(): pl.pallas_call(functools.partial(kernel, dims), out_shape=shapes, in_spec...  49.2 us

profile of v3, /device:TPU:1, one launch (start us, length us, event | category | flops | bytes accessed | tf_op | source)
XLA Modules:
  0.0 50.5 jit_solution(373960206429102260)
XLA Ops:
  0.6 49.2 %shard_map.86 = (f32[12,2048]{1,0:T(8,128)S(1)}, f32[16,128]{1,0:T(8,128)S(1)}) custom-call(bf16[96,128,128]{2,1,0:T(8,128)(2,1)} %refs_0_.1, s32[96]{0:T(128)} %refs_1_.1, s32[1,96]{1,0:T(1,128)} %bitcast.4, f32[12,2048]{1,0:T(8,128)} %refs_3_.1, f32[1,2048]{1,0:T(1,128)} %bitcast.3, f32[12,2048]{1,0:T(8,128)} %refs_5_.1, f32[12,2048]{1,0:T(8,128)} %refs_6_.1), custom_call_target="tpu_custom_call" | custom-call | tf_op jit(solution)/shard_map/pallas_call | solution.py:367
  49.8 0.7 %shard_map.87 = (f32[12,2048]{1,0:T(8,128)}, f32[16,128]{1,0:T(8,128)}) custom-call(f32[12,2048]{1,0:T(8,128)S(1)} %get-tuple-element.6.adj_ref, f32[16,128]{1,0:T(8,128)S(1)} %get-tuple-element.7.grad_ref), custom_call_target="tpu_custom_call" | custom-call | tf_op jit(solution)/shard_map/pallas_call | solution.py:406
